TPU v7x, 32 devices: a whole 2x2x4 slice. The times are simulated.
32 devices in a mesh: pipe: 4 (over y, x), dp: 8 (over z, core).
Axes of the slice: x: 2, y: 2, z: 4, core: 2. Of those that a mesh axis runs over, the one named last changes fastest.
Arguments:
- hidden: float32 [64, 2048], P('dp', 'pipe'), may hold values from -6 to 6
- weight: float32 [8192, 2048], P(('pipe', 'dp')), may hold values from -0.375 to 0.375
- log_norm: float32 [64], replicated, may hold values from 14 to 17
- targets: int32 [64], replicated, may hold values from 0 to 8191
- loss_grad: float32 [64], replicated, may hold values from 0.5 to 2
Outputs:
- grad_hidden: float32 [64, 2048], P('dp', 'pipe')
- grad_weight: float32 [8192, 2048], P(('pipe', 'dp'))
All inputs are finite; a program needn't handle non-finite values.
Results may differ from a plain program's by a relative error of at most 0.0003.
Values sent between devices are 32-bit elements; how exact they have to be, the bound alone decides.
A program may use at most 64 MiB of HBM per device.

v0:
```python
import jax
import jax.numpy as jnp
from jax import lax
from jax.sharding import PartitionSpec as P


def on_device(hidden, weight, log_norm, targets, loss_grad):
    vocab_rows = weight.shape[0]
    full_rows = lax.all_gather(hidden, "pipe", axis=1, tiled=True)
    all_tokens = lax.all_gather(full_rows, "dp", axis=0, tiled=True)
    shard_index = lax.axis_index("pipe") * lax.axis_size("dp") + lax.axis_index("dp")
    first_row = shard_index * vocab_rows
    logits = lax.dot_general(
        all_tokens,
        weight,
        (((1,), (1,)), ((), ())),
        precision=lax.Precision.HIGHEST,
        preferred_element_type=jnp.float32,
    )
    prob = jnp.exp(logits - log_norm[:, None])
    columns = first_row + jnp.arange(vocab_rows, dtype=jnp.int32)
    onehot = (targets[:, None] == columns[None, :]).astype(jnp.float32)
    dlogits = loss_grad[:, None] * (prob - onehot)
    grad_weight = lax.dot_general(
        dlogits,
        all_tokens,
        (((0,), (0,)), ((), ())),
        precision=lax.Precision.HIGHEST,
        preferred_element_type=jnp.float32,
    )
    token_part = lax.psum_scatter(
        jnp.dot(
            dlogits, weight, precision=lax.Precision.HIGHEST, preferred_element_type=jnp.float32
        ),
        "dp",
        scatter_dimension=0,
        tiled=True,
    )
    grad_hidden = lax.psum_scatter(token_part, "pipe", scatter_dimension=1, tiled=True)
    return (grad_hidden, grad_weight)


def solution(mesh):
    in_specs = (P("dp", "pipe"), P(("pipe", "dp"), None), P(), P(), P())
    out_specs = (P("dp", "pipe"), P(("pipe", "dp"), None))
    return jax.shard_map(
        on_device, mesh=mesh, in_specs=in_specs, out_specs=out_specs, check_vma=False
    )
```

profile of v0, /device:TPU:0, one launch (start us, length us, event | category | flops | bytes accessed | tf_op | source)
XLA Modules:
  0.0 100.7 jit_solution(5292879912214681538)
XLA Ops:
  7.2 0.0 copy-start
  7.2 0.0 reduce-scatter.3.cloned.1.call-start
  7.2 10.0 %all_gather.6 = f32[8,2048]{1,0:T(8,128)S(1)} all-gather(f32[8,512]{1,0:T(8,128)} %param.5), channel_id=1, replica_groups=mesh['pipe'=4,'dp'=8] {'pipe'}, dimensions={1}, use_global_device_ids=true | all-gather | bytes 81920 | tf_op jit(solution)/shard_map/all_gather | solution.py:9
  17.2 15.4 %all_gather.7 = f32[64,2048]{1,0:T(8,128)S(1)} all-gather(f32[8,2048]{1,0:T(8,128)S(1)} %all_gather.6), channel_id=1, replica_groups=mesh['pipe'=4,'dp'=8] {'dp'}, dimensions={0}, use_global_device_ids=true | all-gather | bytes 589824 | tf_op jit(solution)/shard_map/all_gather | solution.py:10
  32.6 0.0 copy-done
  32.6 2.7 %fusion.2 = f32[64,256]{1,0:T(8,128)S(1)} fusion(f32[64,2048]{1,0:T(8,128)S(1)} %all_gather.7, f32[256,2048]{1,0:T(8,128)S(1)} %copy-done, s32[256]{0:T(256)S(1)} %iota_add_fusion, f32[64]{0:T(128)} %param.7, f32[64]{0:T(128)} %param.9, s32[64]{0:T(128)} %param.8), kind=kOutput, calls=%fused_computation.3 | convolution fusion | flops 402735104 | bytes 2688768 | tf_op jit(solution)/shard_map/dot_general | solution.py:13
  35.4 2.2 %fusion.3 = f32[64,2048]{1,0:T(8,128)} fusion(f32[64,256]{1,0:T(8,128)S(1)} %fusion.2, f32[256,2048]{1,0:T(8,128)S(1)} %copy-done), kind=kOutput, calls=%fused_computation.5 | convolution fusion | flops 402653184 | bytes 2686976 | tf_op jit(solution)/shard_map/dot_general | solution.py:32
  37.5 0.0 reduce-scatter.3.cloned.1.call-update
  37.6 0.0 reduce-scatter.5.cloned.1.call-start
  37.6 30.8 %reduce-scatter.3.cloned.1.call-done = f32[8,2048]{1,0:T(8,128)} async-done(((f32[64,2048]{1,0:T(8,128)}), f32[8,2048]{1,0:T(8,128)}) %reduce-scatter.3.cloned.1.call-update) | async-done | bytes 65552 | tf_op jit(solution)/shard_map/reduce_scatter | solution.py:31
  68.4 0.0 reduce-scatter.5.cloned.1.call-update
  68.4 3.2 %fusion.4 = f32[256,2048]{1,0:T(8,128)} fusion(f32[64,256]{1,0:T(8,128)S(1)} %fusion.2, f32[64,2048]{1,0:T(8,128)S(1)} %all_gather.7), kind=kOutput, calls=%fused_computation.6 | convolution fusion | flops 402653184 | bytes 2686976 | tf_op jit(solution)/shard_map/dot_general | solution.py:24
  71.6 22.3 %reduce-scatter.5.cloned.1.call-done = f32[8,512]{1,0:T(8,128)} async-done(((f32[8,2048]{1,0:T(8,128)}), f32[8,512]{1,0:T(8,128)}) %reduce-scatter.5.cloned.1.call-update) | async-done | bytes 16400 | tf_op jit(solution)/shard_map/reduce_scatter | solution.py:39
  (1 shorter events, 0.0 us)
Async XLA Ops:
  7.2 25.5 %copy-start = (f32[256,2048]{1,0:T(8,128)S(1)}, f32[256,2048]{1,0:T(8,128)}, u32[]{:S(2)}) copy-start(f32[256,2048]{1,0:T(8,128)} %param.6) | copy-start | bytes 6291460
  7.2 61.2 %reduce-scatter.3.cloned.1.call-start = ((), (), s32[]{:S(2)}) async-start(), calls=%async_computation.2 | async-start | bytes 589824 | tf_op jit(solution)/shard_map/reduce_scatter | solution.py:31
  37.6 56.3 %reduce-scatter.5.cloned.1.call-start = ((), (), s32[]{:S(2)}) async-start(), calls=%async_computation.3 | async-start | bytes 81920 | tf_op jit(solution)/shard_map/reduce_scatter | solution.py:39
Sparse Core Ops, SparseCore 0:
  37.7 30.6 reduce-scatter.2
  71.9 21.9 reduce-scatter.4
where the time goes:
time: 101 us
  waiting for transfers between devices  53.1 us (53%)
  blocking collectives  25.4 us (25%)
  between operations  14.1 us (14%)
  matrix products  8.07 us (8%)
    reduce_scatter x1, waiting for transfers between devices, on_device(): lax.psum_scatter(jnp.dot(dlogits, weight, precision=lax.Precision.HIGHEST...  30.8 us
    reduce_scatter x1, waiting for transfers between devices, on_device(): lax.psum_scatter(token_part, 'pipe', scatter_dimension=1, tiled=True)  22.3 us
    all_gather x1, blocking collectives, on_device(): all_tokens = lax.all_gather(full_rows, 'dp', axis=0, tiled=True)  15.4 us
    all_gather x1, blocking collectives, on_device(): full_rows = lax.all_gather(hidden, 'pipe', axis=1, tiled=True)  9.98 us
    dot_general x1, matrix products, on_device(): lax.dot_general(dlogits, all_tokens, (((0,), (0,)), ((), ())), precision=...  3.16 us
    dot_general x1, matrix products, on_device(): lax.dot_general(all_tokens, weight, (((1,), (1,)), ((), ())), precision=l...  2.73 us
    dot_general x1, matrix products, on_device(): jnp.dot(dlogits, weight, precision=lax.Precision.HIGHEST, preferred_eleme...  2.17 us
  transfers between devices with their start and end apart: 2, of which 2 were waited for; matrix products, arithmetic and copies ran while one was open for 3% of the time, Pallas kernels for 0%

commit v1 on v0

v1 whole, which is shorter than its diff:
```python
import functools

import jax
import jax.numpy as jnp
from jax import lax
from jax.experimental import pallas as pl
from jax.experimental.pallas import tpu as pltpu
from jax.sharding import PartitionSpec as P

F32, BF16 = jnp.float32, jnp.bfloat16
NT = (((1,), (1,)), ((), ()))


def partner(index, k, n):
    if n & (n - 1):
        return lax.rem(index + k, n)
    bit, out = 1, index
    while bit < n:
        if k & bit:
            out = out + bit - 2 * bit * lax.rem(index // bit, 2)
        bit *= 2
    return out


def source(index, k, n):
    if n & (n - 1):
        return lax.rem(index + n - k, n)
    return partner(index, k, n)


def split(x):
    high = x.astype(BF16)
    return high, (x - high.astype(F32)).astype(BF16)


def kernel(
    n_pipe, n_z, h_ref, w_hbm, ln_ref, tg_ref, lg_ref, gh_ref, gw_hbm,
    w_f32, w_hi, w_lo, hid, part, from_core, to_pipe, from_pipe, to_z, from_z, gw,
    w_sem, z_send, z_recv, p_send, p_recv, c_send, c_recv,
    rc_send, rc_recv, rp_send, rp_recv, rz_send, rz_recv, gw_sem,
):
    rows, feat = h_ref.shape
    vocab = w_hbm.shape[0]
    tokens = n_z * 2 * rows
    per_z = (n_pipe - 1) * n_z <= 64
    pipe, dp = lax.axis_index("pipe"), lax.axis_index("dp")
    z, core = dp // 2, lax.rem(dp, 2)
    other = 1 - core

    def at_z(k):
        return {"dp": partner(z, k, n_z) * 2 + core}

    def at_pipe(k):
        return {"pipe": partner(pipe, k, n_pipe)}

    sibling = {"dp": z * 2 + other}

    def remote(src, dst, send, recv, where):
        return pltpu.make_async_remote_copy(
            src_ref=src, dst_ref=dst, send_sem=send, recv_sem=recv, device_id=where,
            device_id_type=pl.DeviceIdType.MESH,
        )

    barrier = pltpu.get_barrier_semaphore()
    peers = [at_z(k) for k in range(1, n_z)] + [at_pipe(k) for k in range(1, n_pipe)] + [sibling]
    for peer in peers:
        pl.semaphore_signal(barrier, inc=1, device_id=peer, device_id_type=pl.DeviceIdType.MESH)
    w_copies = []
    for q in range(n_pipe):
        copy = pltpu.make_async_copy(w_hbm.at[:, pl.ds(q * feat, feat)], w_f32.at[q], w_sem.at[q])
        copy.start()
        w_copies.append(copy)
    hid[pipe, z, core] = h_ref[...]
    pl.semaphore_wait(barrier, len(peers))

    sends = []
    for k in range(1, n_z):
        block = hid.at[pipe, z, core]
        copy = remote(block, block, z_send.at[k], z_recv.at[k], at_z(k))
        copy.start()
        sends.append(copy)

    def over_pipe(j):
        for k in range(1, n_pipe):
            block = hid.at[pipe, source(z, j, n_z), core] if per_z else hid.at[pipe, :, core]
            copy = remote(block, block, p_send.at[k, j], p_recv.at[k, j], at_pipe(k))
            copy.start()
            sends.append(copy)

    def got_z(k):
        block = hid.at[pipe, source(z, k, n_z), core]
        remote(block, block, z_send.at[k], z_recv.at[k], at_z(k)).wait_recv()

    if per_z:
        over_pipe(0)
    for k in range(1, n_z):
        got_z(k)
        if per_z:
            over_pipe(k)
    if not per_z:
        over_pipe(0)

    def to_sibling(k):
        block = hid.at[source(pipe, k, n_pipe), :, core]
        copy = remote(block, block, c_send.at[k], c_recv.at[k], sibling)
        copy.start()
        sends.append(copy)

    to_sibling(0)
    for q in range(n_pipe):
        w_copies[q].wait()
        high, low = split(w_f32[q])
        w_hi[q] = high
        w_lo[q] = low
    for k in range(1, n_pipe):
        q = source(pipe, k, n_pipe)
        for j in range(n_z if per_z else 1):
            block = hid.at[q, source(z, j, n_z), core] if per_z else hid.at[q, :, core]
            remote(block, block, p_send.at[k, j], p_recv.at[k, j], at_pipe(k)).wait_recv()
        to_sibling(k)

    both = jnp.zeros((vocab, 2 * tokens), F32)
    low_part = jnp.zeros((vocab, tokens), F32)
    for k in range(n_pipe):
        q = source(pipe, k, n_pipe)
        block = hid.at[q, :, other]
        remote(block, block, c_send.at[k], c_recv.at[k], sibling).wait_recv()
        high, low = split(hid[q].reshape(tokens, feat))
        both += lax.dot_general(w_hi[q], jnp.concatenate([high, low], 0), NT, preferred_element_type=F32)
        low_part += lax.dot_general(w_lo[q], high, NT, preferred_element_type=F32)
    logits = both[:, :tokens] + both[:, tokens:] + low_part

    first = (pipe * n_z * 2 + dp) * vocab
    column = first + lax.broadcasted_iota(jnp.int32, (vocab, tokens), 0)
    onehot = (column == tg_ref[...]).astype(F32)
    dlogits = lg_ref[...] * (jnp.exp(logits - ln_ref[...]) - onehot)

    d_hi, d_lo = split(dlogits.T)
    d_both = jnp.concatenate([d_hi, d_lo], 0)
    order = list(range(n_pipe - 1, -1, -1))
    core_copies = {}
    for k in order:
        q = partner(pipe, k, n_pipe)
        whole = jnp.dot(d_both, w_hi[q], preferred_element_type=F32)
        total = whole[:tokens] + whole[tokens:] + jnp.dot(d_hi, w_lo[q], preferred_element_type=F32)
        part[k] = total.reshape(n_z, 2, rows, feat)
        copy = remote(part.at[k, :, other], from_core.at[k], rc_send.at[k], rc_recv.at[k], sibling)
        copy.start()
        core_copies[k] = copy
        sends.append(copy)
    pipe_copies = {}
    for k in order:
        core_copies[k].wait_recv()
        to_pipe[k] = part[k, :, core] + from_core[k]
        if k:
            copy = remote(to_pipe.at[k], from_pipe.at[k], rp_send.at[k], rp_recv.at[k], at_pipe(k))
            copy.start()
            pipe_copies[k] = copy
            sends.append(copy)

    t_hi, t_lo = split(dlogits)
    gw_copies = []

    def weight_grad(q):
        high, low = split(hid[q].reshape(tokens, feat))
        gw[q] = (
            jnp.dot(t_hi, high, preferred_element_type=F32)
            + jnp.dot(t_hi, low, preferred_element_type=F32)
            + jnp.dot(t_lo, high, preferred_element_type=F32)
        )
        copy = pltpu.make_async_copy(gw.at[q], gw_hbm.at[:, pl.ds(q * feat, feat)], gw_sem.at[q])
        copy.start()
        gw_copies.append(copy)

    half = (n_pipe + 1) // 2
    for q in range(half):
        weight_grad(q)
    total = to_pipe[0]
    for k in order[:-1]:
        pipe_copies[k].wait_recv()
        total += from_pipe[k]
    to_z[...] = total
    z_copies = []
    for k in range(1, n_z):
        copy = remote(to_z.at[partner(z, k, n_z)], from_z.at[k], rz_send.at[k], rz_recv.at[k], at_z(k))
        copy.start()
        z_copies.append(copy)
        sends.append(copy)
    for q in range(half, n_pipe):
        weight_grad(q)
    mine = to_z[z]
    for k in range(1, n_z):
        z_copies[k - 1].wait_recv()
        mine += from_z[k]
    gh_ref[...] = mine
    for copy in sends:
        copy.wait_send()
    for copy in gw_copies:
        copy.wait()


def on_device(n_pipe, n_dp, hidden, weight, log_norm, targets, loss_grad):
    rows, feat = hidden.shape
    vocab, width = weight.shape
    n_z = n_dp // 2
    dma = pltpu.SemaphoreType.DMA
    n_j = n_z if (n_pipe - 1) * n_z <= 64 else 1
    vmem = pl.BlockSpec(memory_space=pltpu.VMEM)
    hbm = pl.BlockSpec(memory_space=pl.ANY)
    return pl.pallas_call(
        functools.partial(kernel, n_pipe, n_z),
        out_shape=(jax.ShapeDtypeStruct((rows, feat), F32), jax.ShapeDtypeStruct((vocab, width), F32)),
        in_specs=[vmem, hbm, vmem, vmem, vmem],
        out_specs=(vmem, hbm),
        scratch_shapes=[
            pltpu.VMEM((n_pipe, vocab, feat), F32),
            pltpu.VMEM((n_pipe, vocab, feat), BF16),
            pltpu.VMEM((n_pipe, vocab, feat), BF16),
            pltpu.VMEM((n_pipe, n_z, 2, rows, feat), F32),
            pltpu.VMEM((n_pipe, n_z, 2, rows, feat), F32),
            pltpu.VMEM((n_pipe, n_z, rows, feat), F32),
            pltpu.VMEM((n_pipe, n_z, rows, feat), F32),
            pltpu.VMEM((n_pipe, n_z, rows, feat), F32),
            pltpu.VMEM((n_z, rows, feat), F32),
            pltpu.VMEM((n_z, rows, feat), F32),
            pltpu.VMEM((n_pipe, vocab, feat), F32),
            dma((n_pipe,)),
            dma((n_z,)), dma((n_z,)),
            dma((n_pipe, n_j)), dma((n_pipe, n_j)),
            dma((n_pipe,)), dma((n_pipe,)),
            dma((n_pipe,)), dma((n_pipe,)),
            dma((n_pipe,)), dma((n_pipe,)),
            dma((n_z,)), dma((n_z,)),
            dma((n_pipe,)),
        ],
        compiler_params=pltpu.CompilerParams(
            collective_id=0, has_side_effects=True, vmem_limit_bytes=48 * 2**20
        ),
    )(hidden, weight, log_norm[None], targets[None], loss_grad[None])


def solution(mesh):
    in_specs = (P("dp", "pipe"), P(("pipe", "dp"), None), P(), P(), P())
    out_specs = (P("dp", "pipe"), P(("pipe", "dp"), None))
    return jax.shard_map(
        functools.partial(on_device, mesh.shape["pipe"], mesh.shape["dp"]),
        mesh=mesh, in_specs=in_specs, out_specs=out_specs, check_vma=False,
    )
```

time: 101 us -> 32.4 us (0.32)
  waiting for transfers between devices: 53.1 us -> 0 us
  blocking collectives: 25.4 us -> 0 us
  Pallas kernels: 0 us -> 25.3 us
  between operations: 14.1 us -> 0.65 us
  matrix products: 8.07 us -> 0 us
  local copies, waits for them, and re-layouts: 0.01 us -> 6.19 us
    reduce_scatter x2 -> x0, waiting for transfers between devices: 53 us -> none  [the longest x1 30.8 us: on_device(): lax.psum_scatter(jnp.dot(dlogits, weight, precision=lax.Precision.HIGHEST...]
    all_gather x2 -> x0, blocking collectives: 25.4 us -> none  [the longest x1 15.4 us: on_device(): all_tokens = lax.all_gather(full_rows, 'dp', axis=0, tiled=True)]
    pallas_call x0 -> x1, Pallas kernels: none -> 25.3 us  [on_device(): pl.pallas_call(functools.partial(kernel, n_pipe, n_z), out_shape=(jax.Sha...]
    dot_general x3 -> x0, matrix products: 8.07 us -> none  [the longest x1 3.16 us: on_device(): lax.dot_general(dlogits, all_tokens, (((0,), (0,)), ((), ())), precision=...]
    unnamed x2 -> x12, local copies, waits for them, and re-layouts: 0.01 us -> 6.19 us
  transfers between devices with their start and end apart: 2 -> 0, of which waited for: 2 -> 0; matrix products, arithmetic and copies ran while one was open for 3% -> 0% of each run, Pallas kernels for 0% -> 0%
where the time goes in v1:
time: 32.4 us; the launch traced here: 32.2 us
  Pallas kernels  25.3 us (78%)
  local copies, waits for them, and re-layouts  6.19 us (19%)
  between operations  0.65 us (2%)
    pallas_call x1, Pallas kernels, on_device(): pl.pallas_call(functools.partial(kernel, n_pipe, n_z), out_shape=(jax.Sha...  25.3 us
    unnamed x12, local copies, waits for them, and re-layouts  6.19 us

profile of v1, /device:TPU:0, one launch (start us, length us, event | category | flops | bytes accessed | tf_op | source)
XLA Modules:
  0.0 32.2 jit_solution(12884300062535211220)
XLA Ops:
  0.6 0.0 copy-start
  0.6 1.6 %copy-done = f32[256,2048]{1,0:T(8,128)S(1)} copy-done((f32[256,2048]{1,0:T(8,128)S(1)}, f32[256,2048]{1,0:T(8,128)}, u32[]{:S(2)}) %copy-start) | copy-done | bytes 2097176
  2.2 0.0 copy-start.1
  2.2 0.7 %copy-done.1 = f32[8,512]{1,0:T(8,128)S(1)} copy-done((f32[8,512]{1,0:T(8,128)S(1)}, f32[8,512]{1,0:T(8,128)}, u32[]{:S(2)}) %copy-start.1) | copy-done | bytes 16408
  2.9 0.0 copy-start.2
  2.9 0.7 %copy-done.2 = f32[64]{0:T(128)S(1)} copy-done((f32[64]{0:T(128)S(1)}, f32[64]{0:T(128)}, u32[]{:S(2)}) %copy-start.2) | copy-done | bytes 280
  3.6 0.0 copy-start.3
  3.6 0.7 %copy-done.3 = s32[64]{0:T(128)S(1)} copy-done((s32[64]{0:T(128)S(1)}, s32[64]{0:T(128)}, u32[]{:S(2)}) %copy-start.3) | copy-done | bytes 280
  4.3 0.0 copy-start.4
  4.3 0.7 %copy-done.4 = f32[64]{0:T(128)S(1)} copy-done((f32[64]{0:T(128)S(1)}, f32[64]{0:T(128)}, u32[]{:S(2)}) %copy-start.4) | copy-done | bytes 280
  4.9 25.3 %shard_map.68 = (f32[8,512]{1,0:T(8,128)S(1)}, f32[256,2048]{1,0:T(8,128)S(1)}) custom-call(f32[8,512]{1,0:T(8,128)S(1)} %copy-done.1, f32[256,2048]{1,0:T(8,128)S(1)} %copy-done, f32[1,64]{1,0:T(1,128)S(1)} %bitcast.3, s32[1,64]{1,0:T(1,128)S(1)} %bitcast.4, f32[1,64]{1,0:T(1,128)S(1)} %bitcast.5), custom_call_target="tpu_custom_call" | custom-call | tf_op jit(solution)/shard_map/pallas_call | solution.py:210
  30.2 0.6 %copy.9 = f32[8,512]{1,0:T(8,128)} copy(f32[8,512]{1,0:T(8,128)S(1)} %get-tuple-element.4) | data formatting | bytes 32768
  30.8 1.3 %copy.10 = f32[256,2048]{1,0:T(8,128)} copy(f32[256,2048]{1,0:T(8,128)S(1)} %get-tuple-element.5) | data formatting | bytes 4194304
Async XLA Ops:
  0.6 1.6 %copy-start = (f32[256,2048]{1,0:T(8,128)S(1)}, f32[256,2048]{1,0:T(8,128)}, u32[]{:S(2)}) copy-start(f32[256,2048]{1,0:T(8,128)} %w_hbm.1) | copy-start | bytes 6291460
  2.2 0.7 %copy-start.1 = (f32[8,512]{1,0:T(8,128)S(1)}, f32[8,512]{1,0:T(8,128)}, u32[]{:S(2)}) copy-start(f32[8,512]{1,0:T(8,128)} %h_ref.1) | copy-start | bytes 49156
  2.9 0.7 %copy-start.2 = (f32[64]{0:T(128)S(1)}, f32[64]{0:T(128)}, u32[]{:S(2)}) copy-start(f32[64]{0:T(128)} %param.7) | copy-start | bytes 772
  3.6 0.7 %copy-start.3 = (s32[64]{0:T(128)S(1)}, s32[64]{0:T(128)}, u32[]{:S(2)}) copy-start(s32[64]{0:T(128)} %param.8) | copy-start | bytes 772
  4.3 0.7 %copy-start.4 = (f32[64]{0:T(128)S(1)}, f32[64]{0:T(128)}, u32[]{:S(2)}) copy-start(f32[64]{0:T(128)} %param.9) | copy-start | bytes 772

commit v2 on v1

--- a/solution.py
+++ b/solution.py
@@ -34,18 +34,19 @@
 
 
 def kernel(
-    n_pipe, n_z, h_ref, w_hbm, ln_ref, tg_ref, lg_ref, gh_ref, gw_hbm,
-    w_f32, w_hi, w_lo, hid, part, from_core, to_pipe, from_pipe, to_z, from_z, gw,
-    w_sem, z_send, z_recv, p_send, p_recv, c_send, c_recv,
-    rc_send, rc_recv, rp_send, rp_recv, rz_send, rz_recv, gw_sem,
+    n_pipe, n_z, h_hbm, w_hbm, ln_hbm, tg_hbm, lg_hbm, gh_ref, gw,
+    w_f32, w_hi, w_lo, hid, ln_ref, tg_ref, lg_ref, part, from_core, to_pipe, from_pipe, to_z, from_z,
+    w_sem, in_sem, z_send, z_recv, p_send, p_recv, c_send, c_recv,
+    rc_send, rc_recv, rp_send, rp_recv, rz_send, rz_recv,
 ):
-    rows, feat = h_ref.shape
+    rows, feat = h_hbm.shape
     vocab = w_hbm.shape[0]
     tokens = n_z * 2 * rows
     per_z = (n_pipe - 1) * n_z <= 64
     pipe, dp = lax.axis_index("pipe"), lax.axis_index("dp")
     z, core = dp // 2, lax.rem(dp, 2)
     other = 1 - core
+    half = (n_pipe + 1) // 2
 
     def at_z(k):
         return {"dp": partner(z, k, n_z) * 2 + core}
@@ -65,12 +66,19 @@
     peers = [at_z(k) for k in range(1, n_z)] + [at_pipe(k) for k in range(1, n_pipe)] + [sibling]
     for peer in peers:
         pl.semaphore_signal(barrier, inc=1, device_id=peer, device_id_type=pl.DeviceIdType.MESH)
+    h_copy = pltpu.make_async_copy(h_hbm, hid.at[pipe, z, core], in_sem.at[0])
+    h_copy.start()
     w_copies = []
     for q in range(n_pipe):
         copy = pltpu.make_async_copy(w_hbm.at[:, pl.ds(q * feat, feat)], w_f32.at[q], w_sem.at[q])
         copy.start()
         w_copies.append(copy)
-    hid[pipe, z, core] = h_ref[...]
+    small_copies = []
+    for i, (src, dst) in enumerate(((ln_hbm, ln_ref), (tg_hbm, tg_ref), (lg_hbm, lg_ref))):
+        copy = pltpu.make_async_copy(src, dst, in_sem.at[i + 1])
+        copy.start()
+        small_copies.append(copy)
+    h_copy.wait()
     pl.semaphore_wait(barrier, len(peers))
 
     sends = []
@@ -91,8 +99,16 @@
         block = hid.at[pipe, source(z, k, n_z), core]
         remote(block, block, z_send.at[k], z_recv.at[k], at_z(k)).wait_recv()
 
+    def split_weight(q):
+        w_copies[q].wait()
+        high, low = split(w_f32[q])
+        w_hi[q] = high
+        w_lo[q] = low
+
     if per_z:
         over_pipe(0)
+    for q in range(half):
+        split_weight(q)
     for k in range(1, n_z):
         got_z(k)
         if per_z:
@@ -107,11 +123,10 @@
         sends.append(copy)
 
     to_sibling(0)
-    for q in range(n_pipe):
-        w_copies[q].wait()
-        high, low = split(w_f32[q])
-        w_hi[q] = high
-        w_lo[q] = low
+    for q in range(half, n_pipe):
+        split_weight(q)
+    for copy in small_copies:
+        copy.wait()
     for k in range(1, n_pipe):
         q = source(pipe, k, n_pipe)
         for j in range(n_z if per_z else 1):
@@ -159,7 +174,6 @@
             sends.append(copy)
 
     t_hi, t_lo = split(dlogits)
-    gw_copies = []
 
     def weight_grad(q):
         high, low = split(hid[q].reshape(tokens, feat))
@@ -168,11 +182,7 @@
             + jnp.dot(t_hi, low, preferred_element_type=F32)
             + jnp.dot(t_lo, high, preferred_element_type=F32)
         )
-        copy = pltpu.make_async_copy(gw.at[q], gw_hbm.at[:, pl.ds(q * feat, feat)], gw_sem.at[q])
-        copy.start()
-        gw_copies.append(copy)
-
-    half = (n_pipe + 1) // 2
+
     for q in range(half):
         weight_grad(q)
     total = to_pipe[0]
@@ -195,48 +205,75 @@
     gh_ref[...] = mine
     for copy in sends:
         copy.wait_send()
-    for copy in gw_copies:
+
+
+def store_kernel(n_pipe, gh_ref, gw_ref, gh_hbm, gw_hbm, sem):
+    feat = gw_ref.shape[2]
+    copies = [
+        pltpu.make_async_copy(gw_ref.at[q], gw_hbm.at[:, pl.ds(q * feat, feat)], sem.at[q]) for q in range(n_pipe)
+    ]
+    copies.append(pltpu.make_async_copy(gh_ref, gh_hbm, sem.at[n_pipe]))
+    for copy in copies:
+        copy.start()
+    for copy in copies:
         copy.wait()
+
+
+def in_hbm(x):
+    return pltpu.with_memory_space_constraint(x, pltpu.HBM)
+
+
+def in_vmem(x):
+    return pltpu.with_memory_space_constraint(x, pltpu.VMEM)
 
 
 def on_device(n_pipe, n_dp, hidden, weight, log_norm, targets, loss_grad):
     rows, feat = hidden.shape
     vocab, width = weight.shape
     n_z = n_dp // 2
+    tokens = n_dp * rows
     dma = pltpu.SemaphoreType.DMA
     n_j = n_z if (n_pipe - 1) * n_z <= 64 else 1
     vmem = pl.BlockSpec(memory_space=pltpu.VMEM)
-    hbm = pl.BlockSpec(memory_space=pl.ANY)
-    return pl.pallas_call(
+    hbm = pl.BlockSpec(memory_space=pltpu.HBM)
+    hidden_grad, weight_grad = pl.pallas_call(
         functools.partial(kernel, n_pipe, n_z),
-        out_shape=(jax.ShapeDtypeStruct((rows, feat), F32), jax.ShapeDtypeStruct((vocab, width), F32)),
-        in_specs=[vmem, hbm, vmem, vmem, vmem],
-        out_specs=(vmem, hbm),
+        out_shape=(pltpu.VMEM((rows, feat), F32), pltpu.VMEM((n_pipe, vocab, feat), F32)),
+        in_specs=[hbm] * 5,
+        out_specs=(vmem, vmem),
         scratch_shapes=[
             pltpu.VMEM((n_pipe, vocab, feat), F32),
             pltpu.VMEM((n_pipe, vocab, feat), BF16),
             pltpu.VMEM((n_pipe, vocab, feat), BF16),
             pltpu.VMEM((n_pipe, n_z, 2, rows, feat), F32),
+            pltpu.VMEM((1, tokens), F32),
+            pltpu.VMEM((1, tokens), jnp.int32),
+            pltpu.VMEM((1, tokens), F32),
             pltpu.VMEM((n_pipe, n_z, 2, rows, feat), F32),
             pltpu.VMEM((n_pipe, n_z, rows, feat), F32),
             pltpu.VMEM((n_pipe, n_z, rows, feat), F32),
             pltpu.VMEM((n_pipe, n_z, rows, feat), F32),
             pltpu.VMEM((n_z, rows, feat), F32),
             pltpu.VMEM((n_z, rows, feat), F32),
-            pltpu.VMEM((n_pipe, vocab, feat), F32),
-            dma((n_pipe,)),
+            dma((n_pipe,)), dma((4,)),
             dma((n_z,)), dma((n_z,)),
             dma((n_pipe, n_j)), dma((n_pipe, n_j)),
             dma((n_pipe,)), dma((n_pipe,)),
             dma((n_pipe,)), dma((n_pipe,)),
             dma((n_pipe,)), dma((n_pipe,)),
             dma((n_z,)), dma((n_z,)),
-            dma((n_pipe,)),
         ],
         compiler_params=pltpu.CompilerParams(
-            collective_id=0, has_side_effects=True, vmem_limit_bytes=48 * 2**20
+            collective_id=0, has_side_effects=True, vmem_limit_bytes=32 * 2**20
         ),
-    )(hidden, weight, log_norm[None], targets[None], loss_grad[None])
+    )(*(in_hbm(x) for x in (hidden, weight, log_norm[None], targets[None], loss_grad[None])))
+    return pl.pallas_call(
+        functools.partial(store_kernel, n_pipe),
+        out_shape=(jax.ShapeDtypeStruct((rows, feat), F32), jax.ShapeDtypeStruct((vocab, width), F32)),
+        in_specs=[vmem, vmem],
+        out_specs=(hbm, hbm),
+        scratch_shapes=[dma((n_pipe + 1,))],
+    )(in_vmem(hidden_grad), in_vmem(weight_grad))
 
 
 def solution(mesh):

time: 32.4 us -> 27.6 us (0.85)
  local copies, waits for them, and re-layouts: 6.19 us -> 0 us
  Pallas kernels: 25.3 us -> 26.7 us
    unnamed x12 -> x0, local copies, waits for them, and re-layouts: 6.19 us -> none
    pallas_call x1 -> x2, Pallas kernels: 25.3 us -> 26.7 us  [the longest x1 25.4 us: on_device(): pl.pallas_call(functools.partial(kernel, n_pipe, n_z), out_shape=(pltpu.V...]
where the time goes in v2:
time: 27.6 us; the launch traced here: 27.4 us
  Pallas kernels  26.7 us (97%)
  between operations  0.64 us (2%)
    pallas_call x1, Pallas kernels, on_device(): pl.pallas_call(functools.partial(kernel, n_pipe, n_z), out_shape=(pltpu.V...  25.4 us
    pallas_call x1, Pallas kernels, on_device(): pl.pallas_call(functools.partial(store_kernel, n_pipe), out_shape=(jax.Sh...  1.36 us

profile of v2, /device:TPU:0, one launch (start us, length us, event | category | flops | bytes accessed | tf_op | source)
XLA Modules:
  0.0 27.4 jit_solution(12548256046080555771)
XLA Ops:
  0.6 25.4 %shard_map.68 = (f32[8,512]{1,0:T(8,128)S(1)}, f32[4,256,512]{2,1,0:T(8,128)S(1)}) custom-call(f32[8,512]{1,0:T(8,128)} %h_hbm.1, f32[256,2048]{1,0:T(8,128)} %w_hbm.1, f32[1,64]{1,0:T(1,128)} %bitcast.3, s32[1,64]{1,0:T(1,128)} %bitcast.4, f32[1,64]{1,0:T(1,128)} %bitcast.5), custom_call_target="tpu_custom_call" | custom-call | tf_op jit(solution)/shard_map/pallas_call | solution.py:239
  26.0 1.4 %shard_map.69 = (f32[8,512]{1,0:T(8,128)}, f32[256,2048]{1,0:T(8,128)}) custom-call(f32[8,512]{1,0:T(8,128)S(1)} %get-tuple-element.4.gh_ref, f32[4,256,512]{2,1,0:T(8,128)S(1)} %get-tuple-element.5.gw_ref), custom_call_target="tpu_custom_call" | custom-call | tf_op jit(solution)/shard_map/pallas_call | solution.py:270

commit v3 on v2

--- a/solution.py
+++ b/solution.py
@@ -82,7 +82,7 @@
     pl.semaphore_wait(barrier, len(peers))
 
     sends = []
-    for k in range(1, n_z):
+    for k in range(n_z - 1, 0, -1):
         block = hid.at[pipe, z, core]
         copy = remote(block, block, z_send.at[k], z_recv.at[k], at_z(k))
         copy.start()
@@ -127,19 +127,19 @@
         split_weight(q)
     for copy in small_copies:
         copy.wait()
-    for k in range(1, n_pipe):
-        q = source(pipe, k, n_pipe)
-        for j in range(n_z if per_z else 1):
-            block = hid.at[q, source(z, j, n_z), core] if per_z else hid.at[q, :, core]
-            remote(block, block, p_send.at[k, j], p_recv.at[k, j], at_pipe(k)).wait_recv()
-        to_sibling(k)
-
     both = jnp.zeros((vocab, 2 * tokens), F32)
     low_part = jnp.zeros((vocab, tokens), F32)
-    for k in range(n_pipe):
-        q = source(pipe, k, n_pipe)
+    for k in range(1, n_pipe + 1):
+        if k < n_pipe:
+            q = source(pipe, k, n_pipe)
+            for j in range(n_z if per_z else 1):
+                block = hid.at[q, source(z, j, n_z), core] if per_z else hid.at[q, :, core]
+                remote(block, block, p_send.at[k, j], p_recv.at[k, j], at_pipe(k)).wait_recv()
+            to_sibling(k)
+    for k in range(1, n_pipe + 1):
+        q = source(pipe, k - 1, n_pipe)
         block = hid.at[q, :, other]
-        remote(block, block, c_send.at[k], c_recv.at[k], sibling).wait_recv()
+        remote(block, block, c_send.at[k - 1], c_recv.at[k - 1], sibling).wait_recv()
         high, low = split(hid[q].reshape(tokens, feat))
         both += lax.dot_general(w_hi[q], jnp.concatenate([high, low], 0), NT, preferred_element_type=F32)
         low_part += lax.dot_general(w_lo[q], high, NT, preferred_element_type=F32)
@@ -153,8 +153,21 @@
     d_hi, d_lo = split(dlogits.T)
     d_both = jnp.concatenate([d_hi, d_lo], 0)
     order = list(range(n_pipe - 1, -1, -1))
-    core_copies = {}
-    for k in order:
+    z_order = list(range(n_z - 1, -1, -1)) if per_z else [0]
+    core_copies, pipe_copies = {}, {}
+
+    def on_to_pipe(k):
+        core_copies[k].wait_recv()
+        to_pipe[k] = part[k, :, core] + from_core[k]
+        if k:
+            for j in z_order:
+                piece = (k, partner(z, j, n_z)) if per_z else (k,)
+                copy = remote(to_pipe.at[piece], from_pipe.at[piece], rp_send.at[k, j], rp_recv.at[k, j], at_pipe(k))
+                copy.start()
+                pipe_copies[k, j] = copy
+                sends.append(copy)
+
+    for n, k in enumerate(order):
         q = partner(pipe, k, n_pipe)
         whole = jnp.dot(d_both, w_hi[q], preferred_element_type=F32)
         total = whole[:tokens] + whole[tokens:] + jnp.dot(d_hi, w_lo[q], preferred_element_type=F32)
@@ -163,21 +176,16 @@
         copy.start()
         core_copies[k] = copy
         sends.append(copy)
-    pipe_copies = {}
-    for k in order:
-        core_copies[k].wait_recv()
-        to_pipe[k] = part[k, :, core] + from_core[k]
-        if k:
-            copy = remote(to_pipe.at[k], from_pipe.at[k], rp_send.at[k], rp_recv.at[k], at_pipe(k))
-            copy.start()
-            pipe_copies[k] = copy
-            sends.append(copy)
+        if n >= 2:
+            on_to_pipe(order[n - 2])
+    for k in order[-2:]:
+        on_to_pipe(k)
 
     t_hi, t_lo = split(dlogits)
 
     def weight_grad(q):
         high, low = split(hid[q].reshape(tokens, feat))
-        gw[q] = (
+        gw[:, q * feat : (q + 1) * feat] = (
             jnp.dot(t_hi, high, preferred_element_type=F32)
             + jnp.dot(t_hi, low, preferred_element_type=F32)
             + jnp.dot(t_lo, high, preferred_element_type=F32)
@@ -185,34 +193,37 @@
 
     for q in range(half):
         weight_grad(q)
-    total = to_pipe[0]
-    for k in order[:-1]:
-        pipe_copies[k].wait_recv()
-        total += from_pipe[k]
-    to_z[...] = total
-    z_copies = []
-    for k in range(1, n_z):
-        copy = remote(to_z.at[partner(z, k, n_z)], from_z.at[k], rz_send.at[k], rz_recv.at[k], at_z(k))
-        copy.start()
-        z_copies.append(copy)
-        sends.append(copy)
+    z_copies = {}
+    for j in range(n_z - 1, -1, -1):
+        at = partner(z, j, n_z)
+        total = to_pipe[0, at]
+        for k in order[:-1]:
+            if per_z or j == n_z - 1:
+                pipe_copies[k, j if per_z else 0].wait_recv()
+            total += from_pipe[k, at]
+        to_z[at] = total
+        if j:
+            copy = remote(to_z.at[at], from_z.at[j], rz_send.at[j], rz_recv.at[j], at_z(j))
+            copy.start()
+            z_copies[j] = copy
+            sends.append(copy)
     for q in range(half, n_pipe):
         weight_grad(q)
     mine = to_z[z]
     for k in range(1, n_z):
-        z_copies[k - 1].wait_recv()
+        z_copies[k].wait_recv()
         mine += from_z[k]
     gh_ref[...] = mine
     for copy in sends:
         copy.wait_send()
 
 
-def store_kernel(n_pipe, gh_ref, gw_ref, gh_hbm, gw_hbm, sem):
-    feat = gw_ref.shape[2]
-    copies = [
-        pltpu.make_async_copy(gw_ref.at[q], gw_hbm.at[:, pl.ds(q * feat, feat)], sem.at[q]) for q in range(n_pipe)
-    ]
-    copies.append(pltpu.make_async_copy(gh_ref, gh_hbm, sem.at[n_pipe]))
+def store_kernel(pieces, gh_ref, gw_ref, gh_hbm, gw_hbm, sem):
+    rows = gw_ref.shape[0] // pieces
+    copies = [pltpu.make_async_copy(gh_ref, gh_hbm, sem.at[pieces])]
+    for i in range(pieces):
+        block = pl.ds(i * rows, rows)
+        copies.append(pltpu.make_async_copy(gw_ref.at[block], gw_hbm.at[block], sem.at[i]))
     for copy in copies:
         copy.start()
     for copy in copies:
@@ -232,13 +243,14 @@
     vocab, width = weight.shape
     n_z = n_dp // 2
     tokens = n_dp * rows
+    pieces = 8 if vocab % 64 == 0 else 1
     dma = pltpu.SemaphoreType.DMA
     n_j = n_z if (n_pipe - 1) * n_z <= 64 else 1
     vmem = pl.BlockSpec(memory_space=pltpu.VMEM)
     hbm = pl.BlockSpec(memory_space=pltpu.HBM)
     hidden_grad, weight_grad = pl.pallas_call(
         functools.partial(kernel, n_pipe, n_z),
-        out_shape=(pltpu.VMEM((rows, feat), F32), pltpu.VMEM((n_pipe, vocab, feat), F32)),
+        out_shape=(pltpu.VMEM((rows, feat), F32), pltpu.VMEM((vocab, width), F32)),
         in_specs=[hbm] * 5,
         out_specs=(vmem, vmem),
         scratch_shapes=[
@@ -260,7 +272,7 @@
             dma((n_pipe, n_j)), dma((n_pipe, n_j)),
             dma((n_pipe,)), dma((n_pipe,)),
             dma((n_pipe,)), dma((n_pipe,)),
-            dma((n_pipe,)), dma((n_pipe,)),
+            dma((n_pipe, n_j)), dma((n_pipe, n_j)),
             dma((n_z,)), dma((n_z,)),
         ],
         compiler_params=pltpu.CompilerParams(
@@ -268,11 +280,11 @@
         ),
     )(*(in_hbm(x) for x in (hidden, weight, log_norm[None], targets[None], loss_grad[None])))
     return pl.pallas_call(
-        functools.partial(store_kernel, n_pipe),
+        functools.partial(store_kernel, pieces),
         out_shape=(jax.ShapeDtypeStruct((rows, feat), F32), jax.ShapeDtypeStruct((vocab, width), F32)),
         in_specs=[vmem, vmem],
         out_specs=(hbm, hbm),
-        scratch_shapes=[dma((n_pipe + 1,))],
+        scratch_shapes=[dma((pieces + 1,))],
     )(in_vmem(hidden_grad), in_vmem(weight_grad))
 
 

time: 27.6 us -> 26.7 us (0.967)
  Pallas kernels: 26.7 us -> 25.8 us
    pallas_call x1, Pallas kernels: 25.4 us -> 24.4 us  [on_device(): pl.pallas_call(functools.partial(kernel, n_pipe, n_z), out_shape=(pltpu.V...]
where the time goes in v3:
time: 26.7 us; the launch traced here: 26.4 us
  Pallas kernels  25.8 us (97%)
  between operations  0.64 us (2%)
    pallas_call x1, Pallas kernels, on_device(): pl.pallas_call(functools.partial(kernel, n_pipe, n_z), out_shape=(pltpu.V...  24.4 us
    pallas_call x1, Pallas kernels, on_device(): pl.pallas_call(functools.partial(store_kernel, pieces), out_shape=(jax.Sh...  1.39 us

profile of v3, /device:TPU:0, one launch (start us, length us, event | category | flops | bytes accessed | tf_op | source)
XLA Modules:
  0.0 26.4 jit_solution(9762154943424090001)
XLA Ops:
  0.6 24.4 %shard_map.68 = (f32[8,512]{1,0:T(8,128)S(1)}, f32[256,2048]{1,0:T(8,128)S(1)}) custom-call(f32[8,512]{1,0:T(8,128)} %h_hbm.1, f32[256,2048]{1,0:T(8,128)} %w_hbm.1, f32[1,64]{1,0:T(1,128)} %bitcast.3, s32[1,64]{1,0:T(1,128)} %bitcast.4, f32[1,64]{1,0:T(1,128)} %bitcast.5), custom_call_target="tpu_custom_call" | custom-call | tf_op jit(solution)/shard_map/pallas_call | solution.py:251
  25.0 1.4 %shard_map.69 = (f32[8,512]{1,0:T(8,128)}, f32[256,2048]{1,0:T(8,128)}) custom-call(f32[8,512]{1,0:T(8,128)S(1)} %get-tuple-element.4.gh_ref, f32[256,2048]{1,0:T(8,128)S(1)} %get-tuple-element.5.gw_ref), custom_call_target="tpu_custom_call" | custom-call | tf_op jit(solution)/shard_map/pallas_call | solution.py:282

commit v4 on v3

--- a/solution.py
+++ b/solution.py
@@ -89,7 +89,7 @@
         sends.append(copy)
 
     def over_pipe(j):
-        for k in range(1, n_pipe):
+        for k in range(n_pipe - 1, 0, -1):
             block = hid.at[pipe, source(z, j, n_z), core] if per_z else hid.at[pipe, :, core]
             copy = remote(block, block, p_send.at[k, j], p_recv.at[k, j], at_pipe(k))
             copy.start()

time: 26.7 us -> 26.6 us (level)
  no operation moved by 1% of the time
where the time goes in v4:
time: 26.6 us; the launch traced here: 26.4 us
  Pallas kernels  25.7 us (97%)
  between operations  0.64 us (2%)
    pallas_call x1, Pallas kernels, on_device(): pl.pallas_call(functools.partial(kernel, n_pipe, n_z), out_shape=(pltpu.V...  24.3 us
    pallas_call x1, Pallas kernels, on_device(): pl.pallas_call(functools.partial(store_kernel, pieces), out_shape=(jax.Sh...  1.39 us

profile of v4, /device:TPU:0, one launch (start us, length us, event | category | flops | bytes accessed | tf_op | source)
XLA Modules:
  0.0 26.4 jit_solution(17095086020560831602)
XLA Ops:
  0.6 24.3 %shard_map.68 = (f32[8,512]{1,0:T(8,128)S(1)}, f32[256,2048]{1,0:T(8,128)S(1)}) custom-call(f32[8,512]{1,0:T(8,128)} %h_hbm.1, f32[256,2048]{1,0:T(8,128)} %w_hbm.1, f32[1,64]{1,0:T(1,128)} %bitcast.3, s32[1,64]{1,0:T(1,128)} %bitcast.4, f32[1,64]{1,0:T(1,128)} %bitcast.5), custom_call_target="tpu_custom_call" | custom-call | tf_op jit(solution)/shard_map/pallas_call | solution.py:251
  25.0 1.4 %shard_map.69 = (f32[8,512]{1,0:T(8,128)}, f32[256,2048]{1,0:T(8,128)}) custom-call(f32[8,512]{1,0:T(8,128)S(1)} %get-tuple-element.4.gh_ref, f32[256,2048]{1,0:T(8,128)S(1)} %get-tuple-element.5.gw_ref), custom_call_target="tpu_custom_call" | custom-call | tf_op jit(solution)/shard_map/pallas_call | solution.py:282
